TPU v7x, 32 devices: a whole 2x2x4 slice. The times are simulated.
32 devices in a mesh: chan: 2 (over y), point: 16 (over z, x, core).
Axes of the slice: x: 2, y: 2, z: 4, core: 2. Of those that a mesh axis runs over, the one named last changes fastest.
Arguments:
- images: bfloat16 [32, 4, 4, 256, 256], P('point', None, 'chan'), may hold values from -6 to 6
- beam: bfloat16 [32, 4, 256, 256], P('point'), may hold values from 0.049804688 to 1
- exponent: float32 [4], replicated, may hold values from 0.6 to 1.6
- intersection: int32 [32, 4], P('point'), may hold values from 0 to 127
- counts: int32 [32], P('point'), may hold values from 1 to 4
- owner: int32 [128], replicated, may hold values from 0 to 127, each once
- psf: bfloat16 [4, 2, 256, 256], P('chan'), may hold values from -0.375 to 0.375
Outputs:
- sky_tiles: bfloat16 [128, 4, 256, 256], P('point', 'chan')
Inputs may be any that keep to these rules, and one draw needn't show every extreme that they name: `intersection`: slots at or after counts[p] are ignored. `owner`: each sky tile appears once.
All inputs are finite; a program needn't handle non-finite values.
Results may differ from a plain program's by a relative error of at most 0.0065.
Values may be sent and summed in bfloat16 or wider, within the bound.
No kernel may reach another device: no remote copies, remote signals or barrier semaphores. Data moves between devices by JAX's collectives and lax.ppermute only.
A program may use at most 64 MiB of HBM per device.

v0:
```python
import jax
import jax.numpy as jnp
from jax import lax
from jax.sharding import PartitionSpec as P

weight_floor = 0.05


def all_channel_weights(exponent, logs):

    def weight_step(index, accum):
        power = jnp.exp(exponent[index] * logs)
        return accum + power * power

    return (
        lax.fori_loop(0, exponent.shape[0], weight_step, jnp.zeros(logs.shape, jnp.float32))
        / exponent.shape[0]
    )


def shards(images, beam, exponent, intersection, counts, owner, psf):
    pt_dev, slots, ch_dev, tile = (
        images.shape[0],
        images.shape[1],
        images.shape[2],
        images.shape[3],
    )
    npoint = lax.axis_size("point")
    s_dev = pt_dev * slots
    rows = tile // npoint
    nsky = owner.shape[0]
    chan_pos = lax.axis_index("chan")
    beam_log = jnp.log(beam.reshape(s_dev, tile, tile).astype(jnp.float32))
    own_exp = lax.dynamic_slice_in_dim(exponent, chan_pos * ch_dev, ch_dev)
    powers = jnp.exp(own_exp[None, :, None, None] * beam_log[:, None])
    weighted = (powers * images.reshape(s_dev, ch_dev, tile, tile).astype(jnp.float32)).astype(
        jnp.bfloat16
    )
    weight_send = all_channel_weights(exponent, beam_log)[:, None]
    recv_tiles = lax.all_to_all(weighted, "point", split_axis=2, concat_axis=0, tiled=True)
    recv_weights = lax.all_to_all(weight_send, "point", split_axis=2, concat_axis=0, tiled=True)
    all_ids, all_counts = (
        lax.all_gather(intersection, "point", axis=0, tiled=True),
        lax.all_gather(counts, "point", axis=0, tiled=True),
    )
    live = jnp.arange(slots)[None, :] < all_counts[:, None]
    slot_ids = jnp.where(live, all_ids, nsky).reshape(-1)
    member = slot_ids[None, :] == jnp.arange(nsky)[:, None]
    numer = jnp.dot(
        member.astype(jnp.bfloat16),
        recv_tiles.reshape(npoint * s_dev, ch_dev * rows * tile),
        preferred_element_type=jnp.float32,
    )
    numer = numer.reshape(nsky, ch_dev, rows, tile)
    member_f = member.astype(jnp.float32)
    total = jnp.dot(
        member_f, recv_weights.reshape(npoint * s_dev, rows * tile), precision=lax.Precision.HIGHEST
    )
    floored = jnp.maximum(total, weight_floor).reshape(nsky, 1, rows, tile)
    normal = (numer / floored).astype(jnp.bfloat16)
    right_factor = psf[:, 1]
    left_factor = psf[:, 0]
    ordered = jnp.take(normal, owner, axis=0)
    returned = lax.all_to_all(ordered, "point", split_axis=0, concat_axis=2, tiled=True)
    returned = jnp.einsum(
        "scij,ckj->scik", returned, right_factor, preferred_element_type=jnp.float32
    ).astype(jnp.bfloat16)
    return jnp.einsum(
        "cki,scij->sckj", left_factor, returned, preferred_element_type=jnp.float32
    ).astype(jnp.bfloat16)


def solution(mesh):
    return jax.shard_map(
        shards,
        mesh=mesh,
        in_specs=(
            P("point", None, "chan", None, None),
            P("point", None, None, None),
            P(),
            P("point", None),
            P("point"),
            P(),
            P("chan", None, None, None),
        ),
        out_specs=P("point", "chan", None, None),
        check_vma=False,
    )
```

profile of v0, /device:TPU:1, one launch (start us, length us, event | category | flops | bytes accessed | tf_op | source)
XLA Modules:
  0.0 224.3 jit_solution(7030466008887404960)
XLA Ops:
  0.0 1.5 convert_log_fusion
  1.5 2.5 %copy.30 = f32[8,256,256]{2,0,1:T(8,128)} copy(f32[8,256,256]{2,1,0:T(8,128)S(1)} %bitcast.64) | data formatting | bytes 4194304 | tf_op jit(solution)/shard_map/log | solution.py:33
  4.1 4.1 %copy.31 = f32[2,4,2,256,256]{4,2,1,0,3:T(2,128)} copy(bf16[2,4,2,256,256]{4,3,2,1,0:T(8,128)(2,1)S(1)} %copy-done) | data formatting | bytes 6291456 | tf_op jit(solution)/shard_map/convert_element_type | solution.py:36
  8.3 6.2 %multiply_convert_fusion = bf16[8,2,256,256]{3,1,0,2:T(2,128)(2,1)} fusion(f32[8,2,256,256]{3,1,0,2:T(2,128)} %bitcast.66, f32[8,256,256]{2,0,1:T(8,128)} %copy.30, f32[2]{0:T(128)S(1)} %dynamic_slice.10), kind=kLoop, calls=%fused_computation.4 | loop fusion | flops 3145728 | bytes 8388616 | tf_op jit(solution)/shard_map/convert_element_type | solution.py:36
  14.5 7.3 %all-to-all-start = ((bf16[8,2,256,256]{3,1,0,2:T(2,128)(2,1)}), bf16[8,2,256,256]{3,1,0,2:T(2,128)(2,1)}, u32[]{:S(2)}, u32[]{:S(2)}) async-start(bf16[8,2,256,256]{3,1,0,2:T(2,128)(2,1)} %multiply_convert_fusion), calls=%async_computation | async-start | bytes 4194304 | tf_op jit(solution)/shard_map/all_to_all | solution.py:40
  21.8 17.0 %while.14 = (s32[]{:T(128)}, f32[8,256,256]{2,1,0:T(8,128)}, f32[4]{0:T(128)S(1)}, f32[8,256,256]{2,1,0:T(8,128)S(1)}, s32[]{:T(128)}, /*index=5*/s32[]{:T(128)}) while((s32[]{:T(128)}, f32[8,256,256]{2,1,0:T(8,128)}, f32[4]{0:T(128)S(1)}, f32[8,256,256]{2,1,0:T(8,128)S(1)}, s32[]{:T(128)}, /*index=5*/s32[]{:T(128)}) %tuple.36), condition=%wide.region_1.0_spmd.clone, body=%wide.region_0.0_spmd.clone.sunk | while | flops 2097155 | bytes 6291551 | solution.py:16
  21.9 0.7 dynamic_slice.13
  22.5 2.4 %select_add_fusion.2 = f32[8,256,256]{2,1,0:T(8,128)} fusion(f32[8,256,256]{2,1,0:T(8,128)} %get-tuple-element.140, f32[8,256,256]{2,1,0:T(8,128)S(1)} %get-tuple-element.148, f32[]{:T(128)} %bitcast.63, pred[]{:T(512)S(6)} %compare.3), kind=kLoop, calls=%fused_computation.1.clone.1 | loop fusion | flops 2097152 | bytes 6291461 | tf_op jit(solution)/shard_map/while/body/eval_jaxpr/add | solution.py:13
  24.9 0.6 dynamic_slice.13
  25.6 4.0 %select_add_fusion.2 = f32[8,256,256]{2,1,0:T(8,128)} fusion(f32[8,256,256]{2,1,0:T(8,128)} %get-tuple-element.140, f32[8,256,256]{2,1,0:T(8,128)S(1)} %get-tuple-element.148, f32[]{:T(128)} %bitcast.63, pred[]{:T(512)S(6)} %compare.3), kind=kLoop, calls=%fused_computation.1.clone.1 | loop fusion | flops 2097152 | bytes 6291461 | tf_op jit(solution)/shard_map/while/body/eval_jaxpr/add | solution.py:13
  30.2 4.0 %select_add_fusion.2 = f32[8,256,256]{2,1,0:T(8,128)} fusion(f32[8,256,256]{2,1,0:T(8,128)} %get-tuple-element.140, f32[8,256,256]{2,1,0:T(8,128)S(1)} %get-tuple-element.148, f32[]{:T(128)} %bitcast.63, pred[]{:T(512)S(6)} %compare.3), kind=kLoop, calls=%fused_computation.1.clone.1 | loop fusion | flops 2097152 | bytes 6291461 | tf_op jit(solution)/shard_map/while/body/eval_jaxpr/add | solution.py:13
  34.9 4.0 %select_add_fusion.2 = f32[8,256,256]{2,1,0:T(8,128)} fusion(f32[8,256,256]{2,1,0:T(8,128)} %get-tuple-element.140, f32[8,256,256]{2,1,0:T(8,128)S(1)} %get-tuple-element.148, f32[]{:T(128)} %bitcast.63, pred[]{:T(512)S(6)} %compare.3), kind=kLoop, calls=%fused_computation.1.clone.1 | loop fusion | flops 2097152 | bytes 6291461 | tf_op jit(solution)/shard_map/while/body/eval_jaxpr/add | solution.py:13
  38.9 4.3 %fusion.4 = f32[8,1,256,256]{3,0,1,2:T(8,128)} fusion(f32[8,256,256]{2,1,0:T(8,128)} %get-tuple-element.84), kind=kLoop, calls=%fused_computation.12 | loop fusion | flops 524288 | bytes 4194304 | tf_op jit(solution)/shard_map/broadcast_in_dim | solution.py:39
  43.1 20.3 %all-to-all-done = bf16[8,2,256,256]{3,1,0,2:T(2,128)(2,1)} async-done(((bf16[8,2,256,256]{3,1,0,2:T(2,128)(2,1)}), bf16[8,2,256,256]{3,1,0,2:T(2,128)(2,1)}, u32[]{:S(2)}, u32[]{:S(2)}) %all-to-all-start) | async-done | bytes 2097184 | tf_op jit(solution)/shard_map/all_to_all | solution.py:40
  63.4 10.9 %all-to-all-start.1 = ((f32[8,1,256,256]{3,0,1,2:T(8,128)}), f32[8,1,256,256]{3,0,1,2:T(8,128)S(1)}, u32[]{:S(2)}, u32[]{:S(2)}) async-start(f32[8,1,256,256]{3,0,1,2:T(8,128)} %fusion.4), calls=%async_computation.1 | async-start | bytes 4194304 | tf_op jit(solution)/shard_map/all_to_all | solution.py:41
  75.8 46.7 %all-reduce = s32[32]{0:T(128)S(1)} all-reduce(s32[32]{0:T(128)S(1)} %dynamic-update-slice), channel_id=1, replica_groups=mesh['chan'=2,'point'=16] {'point'}, use_global_device_ids=true, to_apply=%add | all-reduce | flops 32 | bytes 256
  122.5 20.5 %all-gather = s32[16,2,4]{2,1,0:T(2,128)S(1)} all-gather(s32[1,2,4]{2,1,0:T(2,128)S(1)} %bitcast.78), channel_id=1, replica_groups=mesh['chan'=2,'point'=16] {'point'}, dimensions={0}, use_global_device_ids=true | all-gather | bytes 544 | tf_op jit(solution)/shard_map/all_gather | solution.py:43
  143.2 2.3 %copy.32 = bf16[8,2,256,256]{3,2,1,0:T(8,128)(2,1)S(1)} copy(bf16[8,2,256,256]{3,1,0,2:T(2,128)(2,1)} %all-to-all-done) | data formatting | bytes 4194304 | tf_op jit(solution)/shard_map/all_to_all | solution.py:40
  145.6 1.6 copy.33
  147.2 4.2 %reshape.32 = bf16[128,8192]{1,0:T(8,128)(2,1)} reshape(bf16[16,8,2,16,256]{4,3,2,1,0:T(8,128)(2,1)} %copy.33) | data formatting | bytes 4194304 | tf_op jit(solution)/shard_map/reshape | solution.py:51
  151.4 4.1 %copy.34 = bf16[8192,128]{1,0:T(8,128)(2,1)} copy(bf16[8192,128]{0,1:T(8,128)(2,1)} %bitcast.69) | data formatting | bytes 4194304 | tf_op jit(solution)/shard_map/dot_general | solution.py:49
  155.5 0.7 copy.67
  156.1 1.6 copy.52
  157.8 1.2 convolution_maximum_fusion
  159.2 1.4 copy-done.1
  160.6 0.7 divide_convert_fusion
  161.3 2.5 %copy.38 = bf16[128,2,16,256]{3,2,1,0:T(8,128)(2,1)} copy(bf16[128,2,16,256]{3,0,2,1:T(8,128)(2,1)S(1)} %divide_convert_fusion) | data formatting | bytes 4194304 | tf_op jit(solution)/shard_map/convert_element_type | solution.py:60
  163.8 2.3 %gather_fusion = bf16[128,2,16,256]{3,2,1,0:T(8,128)(2,1)S(1)} fusion(bf16[128,2,16,256]{3,2,1,0:T(8,128)(2,1)} %copy.38, s32[1024]{0:T(1024)S(1)} %pad_clamp_fusion), kind=kCustom, calls=%fused_computation | custom fusion | bytes 4194816 | tf_op jit(solution)/shard_map/jit(_take)/gather | solution.py:63
  166.4 50.4 %all_to_all.48 = bf16[128,2,16,256]{3,2,1,0:T(8,128)(2,1)S(1)} all-to-all(bf16[128,2,16,256]{3,2,1,0:T(8,128)(2,1)S(1)} %broadcast_select_fusion), channel_id=1, replica_groups=mesh['chan'=2,'point'=16] {'point'}, dimensions={0} | all-to-all | bytes 4194304 | tf_op jit(solution)/shard_map/all_to_all | solution.py:64
  217.0 0.8 copy-done.3
  217.8 2.6 %convert_bitcast_fusion = bf16[8,2,256,256]{2,3,0,1:T(8,128)(2,1)} fusion(bf16[8,2,256,256]{3,2,1,0:T(8,128)(2,1)S(1)} %bitcast.76, bf16[2,2,256,256]{3,2,1,0:T(8,128)(2,1)S(1)} %copy-done.3), kind=kOutput, calls=%fused_computation.13 | convolution fusion | flops 1075838976 | bytes 4718592 | tf_op jit(solution)/shard_map/cki,scij->sckj/dot_general | solution.py:68
  220.4 3.9 %copy.44 = bf16[8,2,256,256]{3,2,1,0:T(8,128)(2,1)} copy(bf16[8,2,256,256]{2,3,0,1:T(8,128)(2,1)} %convert_bitcast_fusion) | data formatting | bytes 4194304 | tf_op jit(solution)/shard_map/convert_element_type | solution.py:70
  (30 shorter events, 3.1 us)
Async XLA Ops:
  1.5 2.6 %copy-start = (bf16[2,4,2,256,256]{4,3,2,1,0:T(8,128)(2,1)S(1)}, bf16[2,4,2,256,256]{4,3,2,1,0:T(8,128)(2,1)}, u32[]{:S(2)}) copy-start(bf16[2,4,2,256,256]{4,3,2,1,0:T(8,128)(2,1)} %param.9) | copy-start | bytes 6291460
  4.1 4.1 %copy-start.4 = (f32[4]{0:T(128)S(1)}, f32[4]{0:T(128)}, u32[]{:S(2)}) copy-start(f32[4]{0:T(128)} %param.11) | copy-start | bytes 52
  14.5 48.9 %all-to-all-start = ((bf16[8,2,256,256]{3,1,0,2:T(2,128)(2,1)}), bf16[8,2,256,256]{3,1,0,2:T(2,128)(2,1)}, u32[]{:S(2)}, u32[]{:S(2)}) async-start(bf16[8,2,256,256]{3,1,0,2:T(2,128)(2,1)} %multiply_convert_fusion), calls=%async_computation | async-start | bytes 4194304 | tf_op jit(solution)/shard_map/all_to_all | solution.py:40
  43.1 31.2 %copy-start.7 = (u32[32]{0:T(128)S(1)}, u32[32]{0:T(128)}, u32[]{:S(2)}) copy-start(u32[32]{0:T(128)} %constant.62) | copy-start | bytes 388
  43.1 32.4 %copy-start.5 = (s32[2]{0:T(128)S(1)}, s32[2]{0:T(128)}, u32[]{:S(2)}) copy-start(s32[2]{0:T(128)} %param.13) | copy-start | bytes 28
  43.1 79.3 %copy-start.2 = (s32[2,4]{1,0:T(2,128)S(1)}, s32[2,4]{1,0:T(2,128)}, u32[]{:S(2)}) copy-start(s32[2,4]{1,0:T(2,128)} %param.12) | copy-start | bytes 100
  43.1 100.1 %copy-start.6 = (s32[128]{0:T(128)S(1)}, s32[128]{0:T(128)}, u32[]{:S(2)}) copy-start(s32[128]{0:T(128)} %param.14) | copy-start | bytes 1540
  63.4 92.0 %all-to-all-start.1 = ((f32[8,1,256,256]{3,0,1,2:T(8,128)}), f32[8,1,256,256]{3,0,1,2:T(8,128)S(1)}, u32[]{:S(2)}, u32[]{:S(2)}) async-start(f32[8,1,256,256]{3,0,1,2:T(8,128)} %fusion.4), calls=%async_computation.1 | async-start | bytes 4194304 | tf_op jit(solution)/shard_map/all_to_all | solution.py:41
  159.0 1.6 copy-start.1
  216.8 1.0 copy-start.3
where the time goes:
time: 225 us; the launch traced here: 224 us
  blocking collectives  118 us (52%)
  local copies, waits for them, and re-layouts  36.1 us (16%)
  other arithmetic  26.8 us (12%)
  waiting for transfers between devices  20.3 us (9%)
  starting transfers between devices  18.2 us (8%)
  matrix products  4.58 us (2%)
    all_to_all x1, blocking collectives, shards(): lax.all_to_all(ordered, 'point', split_axis=0, concat_axis=2, tiled=True)  50.4 us
    unnamed x1, blocking collectives  46.7 us
    all_gather x1, blocking collectives, shards(): lax.all_gather(intersection, 'point', axis=0, tiled=True)  20.5 us
    all_to_all x1, waiting for transfers between devices, shards(): lax.all_to_all(weighted, 'point', split_axis=2, concat_axis=0, tiled=True)  20.3 us
    add x4, other arithmetic, weight_step(): return accum + power * power  14.4 us
    all_to_all x1, starting transfers between devices, shards(): lax.all_to_all(weight_send, 'point', split_axis=2, concat_axis=0, tiled=T...  10.9 us
    all_to_all x1, starting transfers between devices, shards(): lax.all_to_all(weighted, 'point', split_axis=2, concat_axis=0, tiled=True)  7.32 us
    convert_element_type x1, other arithmetic, shards(): (powers * images.reshape(s_dev, ch_dev, tile, tile).astype(jnp.float32))....  6.24 us
  transfers between devices with their start and end apart: 2, of which 1 were waited for; matrix products, arithmetic and copies ran while one was open for 15% of the time, Pallas kernels for 0%

commit v1 on v0

v1 whole, which is shorter than its diff:
```python
import functools

import jax
import jax.numpy as jnp
from jax import lax
from jax.experimental import pallas as pl
from jax.experimental.pallas import tpu as pltpu
from jax.sharding import PartitionSpec as P

weight_floor = 0.05
VMEM_LIMIT = 48 * 1024 * 1024


def params():
    return pltpu.CompilerParams(vmem_limit_bytes=VMEM_LIMIT)


def put_rows(out_ref, at, value):
    group, rows = out_ref.shape[0], out_ref.shape[-2]
    for g in range(group):
        out_ref[(g,) + at] = value[g * rows:(g + 1) * rows].astype(jnp.bfloat16)


def row_block(tile, npoint):
    rows = tile // npoint
    block = max(rows, 16)
    return rows, block, block // rows


def weight_body(exp_ref, images_ref, beam_ref, out_ref):
    slots = images_ref.shape[1]
    for p in range(images_ref.shape[0]):
        for s in range(slots):
            logs = jnp.log(beam_ref[p, s].astype(jnp.float32))
            for c in range(images_ref.shape[2]):
                power = jnp.exp(exp_ref[c] * logs)
                plane = images_ref[p, s, c].astype(jnp.float32)
                put_rows(out_ref, (p * slots + s, c), power * plane)


def weigh(own_exp, images, beam, npoint):
    pts, slots, ch, tile, _ = images.shape
    rows, block, group = row_block(tile, npoint)
    return pl.pallas_call(
        weight_body,
        grid=(npoint // group,),
        in_specs=[
            pl.BlockSpec(memory_space=pltpu.SMEM),
            pl.BlockSpec((pts, slots, ch, block, tile), lambda i: (0, 0, 0, i, 0)),
            pl.BlockSpec((pts, slots, block, tile), lambda i: (0, 0, i, 0)),
        ],
        out_specs=pl.BlockSpec((group, pts * slots, ch, rows, tile), lambda i: (i, 0, 0, 0, 0)),
        out_shape=jax.ShapeDtypeStruct((npoint, pts * slots, ch, rows, tile), jnp.bfloat16),
        compiler_params=params(),
    )(own_exp, images, beam)


def split_body(beam_ref, out_ref):
    for s in range(beam_ref.shape[0]):
        put_rows(out_ref, (s,), beam_ref[s].astype(jnp.float32))


def split_rows(beam, npoint):
    s, tile, _ = beam.shape
    rows, block, group = row_block(tile, npoint)
    return pl.pallas_call(
        split_body,
        grid=(npoint // group,),
        in_specs=[pl.BlockSpec((s, block, tile), lambda i: (0, i, 0))],
        out_specs=pl.BlockSpec((group, s, rows, tile), lambda i: (i, 0, 0, 0)),
        out_shape=jax.ShapeDtypeStruct((npoint, s, rows, tile), jnp.bfloat16),
        compiler_params=params(),
    )(beam)


def total_body(s_dev, ids_ref, exp_ref, beam_ref, out_ref, acc_ref):
    nchan, npoint, part = beam_ref.shape[:3]
    nsky = out_ref.shape[0]
    ch = exp_ref.shape[0]
    acc_ref[...] = jnp.zeros_like(acc_ref)

    def step(d, carry):
        for share in range(nchan):
            for k in range(part):
                at = ids_ref[d, share * part + k]

                @pl.when(at < nsky)
                def _():
                    logs = jnp.log(beam_ref[share, d, k].astype(jnp.float32))
                    pw = jnp.zeros_like(logs)
                    for c in range(ch):
                        power = jnp.exp(exp_ref[c] * logs)
                        pw = pw + power * power
                    acc_ref[at] += pw * (1.0 / ch)

        return carry

    lax.fori_loop(0, npoint, step, 0)
    out_ref[...] = jnp.maximum(acc_ref[...], weight_floor)


def totals(ids, exponent, beams, nsky):
    rows, tile = beams.shape[3:]
    s_dev = ids.shape[1]
    return pl.pallas_call(
        functools.partial(total_body, s_dev),
        in_specs=[
            pl.BlockSpec(memory_space=pltpu.SMEM),
            pl.BlockSpec(memory_space=pltpu.SMEM),
            pl.BlockSpec(memory_space=pltpu.VMEM),
        ],
        out_specs=pl.BlockSpec(memory_space=pltpu.VMEM),
        out_shape=jax.ShapeDtypeStruct((nsky, rows, tile), jnp.float32),
        scratch_shapes=[pltpu.VMEM((nsky, rows, tile), jnp.float32)],
        compiler_params=params(),
    )(ids, exponent, beams)


def normal_body(ids_ref, owner_ref, tiles_ref, floor_ref, out_ref, acc_ref):
    npoint, s_dev, ch = tiles_ref.shape[:3]
    nsky = floor_ref.shape[0]
    acc_ref[...] = jnp.zeros_like(acc_ref)

    def step(d, carry):
        for s in range(s_dev):
            at = ids_ref[d, s]

            @pl.when(at < nsky)
            def _():
                acc_ref[at] += tiles_ref[d, s].astype(jnp.float32)

        return carry

    lax.fori_loop(0, npoint, step, 0)
    per = out_ref.shape[1]

    def emit(d, carry):
        for k in range(per):
            t = owner_ref[d * per + k]
            inv = floor_ref[t]
            for c in range(ch):
                out_ref[d, k, c] = (acc_ref[t, c] / inv).astype(jnp.bfloat16)
        return carry

    lax.fori_loop(0, npoint, emit, 0)


def normalise(ids, owner, tiles, floored):
    npoint, s_dev, ch, rows, tile = tiles.shape
    nsky = owner.shape[0]
    return pl.pallas_call(
        normal_body,
        in_specs=[
            pl.BlockSpec(memory_space=pltpu.SMEM),
            pl.BlockSpec(memory_space=pltpu.SMEM),
            pl.BlockSpec(memory_space=pltpu.VMEM),
            pl.BlockSpec(memory_space=pltpu.VMEM),
        ],
        out_specs=pl.BlockSpec(memory_space=pltpu.VMEM),
        out_shape=jax.ShapeDtypeStruct((npoint, nsky // npoint, ch, rows, tile), jnp.bfloat16),
        scratch_shapes=[pltpu.VMEM((nsky, ch, rows, tile), jnp.float32)],
        compiler_params=params(),
    )(ids, owner, tiles, floored)


def conv_body(tiles_ref, psf_ref, out_ref):
    tile = psf_ref.shape[-1]
    for c in range(tiles_ref.shape[2]):
        plane = tiles_ref[:, 0, c].reshape(tile, tile)
        left = lax.dot_general(
            plane, psf_ref[c, 1], (((1,), (1,)), ((), ())), preferred_element_type=jnp.float32
        ).astype(jnp.bfloat16)
        out_ref[0, c] = jnp.dot(
            psf_ref[c, 0], left, preferred_element_type=jnp.float32
        ).astype(jnp.bfloat16)


def convolve(tiles, psf):
    npoint, per, ch, rows, tile = tiles.shape
    return pl.pallas_call(
        conv_body,
        grid=(per,),
        in_specs=[
            pl.BlockSpec((npoint, 1, ch, rows, tile), lambda i: (0, i, 0, 0, 0)),
            pl.BlockSpec(psf.shape, lambda i: (0, 0, 0, 0)),
        ],
        out_specs=pl.BlockSpec((1, ch, tile, tile), lambda i: (i, 0, 0, 0)),
        out_shape=jax.ShapeDtypeStruct((per, ch, tile, tile), jnp.bfloat16),
        compiler_params=params(),
    )(tiles, psf)


def shards(images, beam, exponent, intersection, counts, owner, psf):
    pts, slots, ch, tile, _ = images.shape
    npoint = lax.axis_size("point")
    nchan = lax.axis_size("chan")
    s_dev = pts * slots
    part = s_dev // nchan
    nsky = owner.shape[0]
    chan_pos = lax.axis_index("chan")

    live = jnp.arange(slots)[None, :] < counts[:, None]
    own_ids = jnp.where(live, intersection, nsky).reshape(1, s_dev)
    ids = lax.all_to_all(
        jnp.broadcast_to(own_ids, (npoint, s_dev)), "point", split_axis=0, concat_axis=0, tiled=True
    )
    own_beam = lax.dynamic_slice_in_dim(
        beam.reshape(s_dev, tile, tile), chan_pos * part, part, axis=0
    )
    beam_rows = lax.all_to_all(
        split_rows(own_beam, npoint), "point", split_axis=0, concat_axis=0, tiled=True
    )
    own_exp = lax.dynamic_slice_in_dim(exponent, chan_pos * ch, ch)
    weighted = weigh(own_exp, images, beam, npoint)
    tiles = lax.all_to_all(weighted, "point", split_axis=0, concat_axis=0, tiled=True)
    beams = lax.all_gather(beam_rows, "chan", axis=0, tiled=False)
    floored = totals(ids, exponent, beams, nsky)
    ordered = normalise(ids, owner, tiles, floored)
    returned = lax.all_to_all(ordered, "point", split_axis=0, concat_axis=0, tiled=True)
    return convolve(returned, psf)


def solution(mesh):
    return jax.shard_map(
        shards,
        mesh=mesh,
        in_specs=(
            P("point", None, "chan", None, None),
            P("point", None, None, None),
            P(),
            P("point", None),
            P("point"),
            P(),
            P("chan", None, None, None),
        ),
        out_specs=P("point", "chan", None, None),
        check_vma=False,
    )
```

time: 225 us -> 162 us (0.72)
  blocking collectives: 118 us -> 58.5 us
  local copies, waits for them, and re-layouts: 36.1 us -> 5.2 us
  other arithmetic: 26.8 us -> 0.9 us
  waiting for transfers between devices: 20.3 us -> 45.8 us
  Pallas kernels: 0 us -> 21.1 us
  between operations: 0.81 us -> 13.5 us
  matrix products: 4.58 us -> 0 us
    unnamed x1 -> x0, blocking collectives: 46.7 us -> none
    all_gather x0 -> x1, waiting for transfers between devices: none -> 23.8 us  [shards(): beams = lax.all_gather(beam_rows, 'chan', axis=0, tiled=False)]
    pallas_call x0 -> x5, Pallas kernels: none -> 21.1 us  [the longest x1 6.6 us: weigh(): pl.pallas_call(weight_body, grid=(npoint // group,), in_specs=[pl.BlockSp...]
    all_gather x1 -> x0, blocking collectives: 20.5 us -> none  [shards(): lax.all_gather(intersection, 'point', axis=0, tiled=True)]
    add x4 -> x0, other arithmetic: 14.4 us -> none  [weight_step(): return accum + power * power]
    convert_element_type x3 -> x0, local copies, waits for them, and re-layouts: 10.5 us -> none  [the longest x1 4.13 us: shards(): images.reshape(s_dev, ch_dev, tile, tile).astype(jnp.float32)]
    all_to_all x1, blocking collectives: 50.4 us -> 58.5 us  [shards(): lax.all_to_all(ordered, 'point', split_axis=0, concat_axis=0, tiled=True)]
    convert_element_type x1 -> x0, other arithmetic: 6.24 us -> none  [shards(): (powers * images.reshape(s_dev, ch_dev, tile, tile).astype(jnp.float32))....]
  transfers between devices with their start and end apart: 2 -> 4, of which waited for: 1 -> 4; matrix products, arithmetic and copies ran while one was open for 15% -> 1% of each run, Pallas kernels for 0% -> 7%
where the time goes in v1:
time: 162 us; the launch traced here: 161 us
  blocking collectives  58.5 us (36%)
  waiting for transfers between devices  45.8 us (28%)
  Pallas kernels  21.1 us (13%)
  starting transfers between devices  16.5 us (10%)
  between operations  13.5 us (8%)
  local copies, waits for them, and re-layouts  5.2 us (3%)
    all_to_all x1, blocking collectives, shards(): lax.all_to_all(ordered, 'point', split_axis=0, concat_axis=0, tiled=True)  58.5 us
    all_gather x1, waiting for transfers between devices, shards(): beams = lax.all_gather(beam_rows, 'chan', axis=0, tiled=False)  23.8 us
    all_to_all x1, waiting for transfers between devices, shards(): lax.all_to_all(weighted, 'point', split_axis=0, concat_axis=0, tiled=True)  10.4 us
    all_to_all x1, waiting for transfers between devices, shards(): lax.all_to_all(split_rows(own_beam, npoint), 'point', split_axis=0, conca...  7.57 us
    all_to_all x1, starting transfers between devices, shards(): lax.all_to_all(jnp.broadcast_to(own_ids, (npoint, s_dev)), 'point', split...  7.32 us
    pallas_call x1, Pallas kernels, weigh(): pl.pallas_call(weight_body, grid=(npoint // group,), in_specs=[pl.BlockSp...  6.6 us
    pallas_call x1, Pallas kernels, convolve(): pl.pallas_call(conv_body, grid=(per,), in_specs=[pl.BlockSpec((npoint, 1,...  6.36 us
    all_to_all x1, starting transfers between devices, shards(): lax.all_to_all(split_rows(own_beam, npoint), 'point', split_axis=0, conca...  4.69 us
  transfers between devices with their start and end apart: 4, of which 4 were waited for; matrix products, arithmetic and copies ran while one was open for 1% of the time, Pallas kernels for 7%

profile of v1, /device:TPU:1, one launch (start us, length us, event | category | flops | bytes accessed | tf_op | source)
XLA Modules:
  0.0 161.5 jit_solution(16867501312745210103)
XLA Ops:
  6.5 0.0 copy-start.1
  6.5 0.9 compare_select_fusion
  7.4 0.1 broadcast_in_dim.14
  7.5 0.6 broadcast_in_dim.15
  8.1 7.3 %all-to-all-start = ((s32[16,1,8]{2,1,0:T(1,128)}), s32[16,1,8]{2,1,0:T(1,128)S(1)}, u32[]{:S(2)}, u32[]{:S(2)}) async-start(s32[16,1,8]{2,1,0:T(1,128)} %broadcast_in_dim.15), calls=%async_computation | async-start | bytes 16384 | tf_op jit(solution)/shard_map/all_to_all | solution.py:204
  15.5 1.1 constant_dynamic-slice_fusion.beam_ref
  16.5 0.4 shard_map.74
  16.9 0.0 copy-start.3
  16.9 0.8 copy-done.3
  17.7 3.4 %all-to-all-done = s32[16,1,8]{2,1,0:T(1,128)S(1)} async-done(((s32[16,1,8]{2,1,0:T(1,128)}), s32[16,1,8]{2,1,0:T(1,128)S(1)}, u32[]{:S(2)}, u32[]{:S(2)}) %all-to-all-start) | async-done | bytes 544 | tf_op jit(solution)/shard_map/all_to_all | solution.py:204
  21.2 4.7 %all-to-all-start.2 = ((bf16[16,4,16,256]{3,2,1,0:T(8,128)(2,1)}), bf16[16,4,16,256]{3,2,1,0:T(8,128)(2,1)}, u32[]{:S(2)}, u32[]{:S(2)}) async-start(bf16[16,4,16,256]{3,2,1,0:T(8,128)(2,1)} %copy-done.3), calls=%async_computation.2 | async-start | bytes 1048576 | tf_op jit(solution)/shard_map/all_to_all | solution.py:210
  25.9 0.0 copy-done.7
  25.9 0.1 dynamic_slice.6.exp_ref
  25.9 0.0 copy-done.1
  25.9 0.0 copy-done.2
  25.9 6.6 %shard_map.73 = bf16[16,8,2,16,256]{4,3,2,1,0:T(8,128)(2,1)} custom-call(f32[2]{0:T(128)S(1)} %dynamic_slice.6.exp_ref, bf16[2,4,2,256,256]{4,3,2,1,0:T(8,128)(2,1)S(1)} %copy-done.2, bf16[2,4,256,256]{3,2,1,0:T(8,128)(2,1)S(1)} %copy-done.1), custom_call_target="tpu_custom_call" | custom-call | tf_op jit(solution)/shard_map/pallas_call | solution.py:44
  32.5 7.6 %all-to-all-done.2 = bf16[16,4,16,256]{3,2,1,0:T(8,128)(2,1)} async-done(((bf16[16,4,16,256]{3,2,1,0:T(8,128)(2,1)}), bf16[16,4,16,256]{3,2,1,0:T(8,128)(2,1)}, u32[]{:S(2)}, u32[]{:S(2)}) %all-to-all-start.2) | async-done | bytes 524320 | tf_op jit(solution)/shard_map/all_to_all | solution.py:210
  40.1 4.4 %all-to-all-start.1 = ((bf16[16,8,2,16,256]{4,3,2,1,0:T(8,128)(2,1)}), bf16[16,8,2,16,256]{4,3,2,1,0:T(8,128)(2,1)S(1)}, u32[]{:S(2)}, u32[]{:S(2)}) async-start(bf16[16,8,2,16,256]{4,3,2,1,0:T(8,128)(2,1)} %shard_map.73), calls=%async_computation.1 | async-start | bytes 4194304 | tf_op jit(solution)/shard_map/all_to_all | solution.py:215
  44.5 0.0 all-gather.3.cloned.1.call-start
  44.6 0.7 all-gather.3.cloned.1.call-update
  45.3 23.8 %all-gather.3.cloned.1.call-done = bf16[32,4,16,256]{3,2,1,0:T(8,128)(2,1)} async-done(((bf16[16,4,16,256]{3,2,1,0:T(8,128)(2,1)}), bf16[32,4,16,256]{3,2,1,0:T(8,128)(2,1)}) %all-gather.3.cloned.1.call-update) | async-done | bytes 1048592 | tf_op jit(solution)/shard_map/all_gather | solution.py:216
  69.0 1.2 copy-done.4
  70.3 4.0 %shard_map.75.floor_ref = f32[128,16,256]{2,1,0:T(8,128)S(1)} custom-call(s32[16,8]{1,0:T(8,128)S(1)} %bitcast.5, f32[4]{0:T(128)S(1)} %copy-done.7, bf16[2,16,4,16,256]{4,3,2,1,0:T(8,128)(2,1)S(1)} %bitcast.4), custom_call_target="tpu_custom_call" | custom-call | tf_op jit(solution)/shard_map/pallas_call | solution.py:105
  74.3 0.0 copy-start
  74.3 1.3 copy-done
  75.6 10.4 %all-to-all-done.1.tiles_ref = bf16[16,8,2,16,256]{4,3,2,1,0:T(8,128)(2,1)S(1)} async-done(((bf16[16,8,2,16,256]{4,3,2,1,0:T(8,128)(2,1)}), bf16[16,8,2,16,256]{4,3,2,1,0:T(8,128)(2,1)S(1)}, u32[]{:S(2)}, u32[]{:S(2)}) %all-to-all-start.1) | async-done | bytes 2097184 | tf_op jit(solution)/shard_map/all_to_all | solution.py:215
  86.0 0.0 copy-done.6
  86.0 3.8 %shard_map.76 = bf16[16,8,2,16,256]{4,3,2,1,0:T(8,128)(2,1)S(1)} custom-call(s32[16,8]{1,0:T(8,128)S(1)} %bitcast.6, s32[128]{0:T(128)S(1)} %copy-done.6, bf16[16,8,2,16,256]{4,3,2,1,0:T(8,128)(2,1)S(1)} %all-to-all-done.1.tiles_ref, f32[128,16,256]{2,1,0:T(8,128)} %copy-done), custom_call_target="tpu_custom_call" | custom-call | tf_op jit(solution)/shard_map/pallas_call | solution.py:151
  89.8 0.0 copy-start.5
  89.8 58.5 %all_to_all.23.tiles_ref = bf16[16,8,2,16,256]{4,3,2,1,0:T(8,128)(2,1)S(1)} all-to-all(bf16[16,8,2,16,256]{4,3,2,1,0:T(8,128)(2,1)S(1)} %shard_map.76), channel_id=1, replica_groups=mesh['chan'=2,'point'=16] {'point'}, dimensions={0} | all-to-all | bytes 4194304 | tf_op jit(solution)/shard_map/all_to_all | solution.py:219
  148.2 0.0 copy-done.5
  148.2 6.4 %shard_map.77 = bf16[8,2,256,256]{3,2,1,0:T(8,128)(2,1)} custom-call(bf16[16,8,2,16,256]{4,3,2,1,0:T(8,128)(2,1)S(1)} %all_to_all.23.tiles_ref, bf16[2,2,256,256]{3,2,1,0:T(8,128)(2,1)S(1)} %copy-done.5), custom_call_target="tpu_custom_call" | custom-call | tf_op jit(solution)/shard_map/pallas_call | solution.py:180
  (4 shorter events, 0.0 us)
Async XLA Ops:
  6.5 19.4 %copy-start.1 = (bf16[2,4,256,256]{3,2,1,0:T(8,128)(2,1)S(1)}, bf16[2,4,256,256]{3,2,1,0:T(8,128)(2,1)}, u32[]{:S(2)}) copy-start(bf16[2,4,256,256]{3,2,1,0:T(8,128)(2,1)} %beam_ref.1) | copy-start | bytes 3145732
  6.5 19.3 %copy-start.7 = (f32[4]{0:T(128)S(1)}, f32[4]{0:T(128)}, u32[]{:S(2)}) copy-start(f32[4]{0:T(128)} %exp_ref.1) | copy-start | bytes 52
  6.5 19.4 %copy-start.2 = (bf16[2,4,2,256,256]{4,3,2,1,0:T(8,128)(2,1)S(1)}, bf16[2,4,2,256,256]{4,3,2,1,0:T(8,128)(2,1)}, u32[]{:S(2)}) copy-start(bf16[2,4,2,256,256]{4,3,2,1,0:T(8,128)(2,1)} %images_ref.1) | copy-start | bytes 6291460
  8.1 13.0 %all-to-all-start = ((s32[16,1,8]{2,1,0:T(1,128)}), s32[16,1,8]{2,1,0:T(1,128)S(1)}, u32[]{:S(2)}, u32[]{:S(2)}) async-start(s32[16,1,8]{2,1,0:T(1,128)} %broadcast_in_dim.15), calls=%async_computation | async-start | bytes 16384 | tf_op jit(solution)/shard_map/all_to_all | solution.py:204
  16.9 0.8 copy-start.3
  21.2 18.9 %all-to-all-start.2 = ((bf16[16,4,16,256]{3,2,1,0:T(8,128)(2,1)}), bf16[16,4,16,256]{3,2,1,0:T(8,128)(2,1)}, u32[]{:S(2)}, u32[]{:S(2)}) async-start(bf16[16,4,16,256]{3,2,1,0:T(8,128)(2,1)} %copy-done.3), calls=%async_computation.2 | async-start | bytes 1048576 | tf_op jit(solution)/shard_map/all_to_all | solution.py:210
  40.1 45.9 %all-to-all-start.1 = ((bf16[16,8,2,16,256]{4,3,2,1,0:T(8,128)(2,1)}), bf16[16,8,2,16,256]{4,3,2,1,0:T(8,128)(2,1)S(1)}, u32[]{:S(2)}, u32[]{:S(2)}) async-start(bf16[16,8,2,16,256]{4,3,2,1,0:T(8,128)(2,1)} %shard_map.73), calls=%async_computation.1 | async-start | bytes 4194304 | tf_op jit(solution)/shard_map/all_to_all | solution.py:215
  44.5 41.5 %copy-start.6 = (s32[128]{0:T(128)S(1)}, s32[128]{0:T(128)}, u32[]{:S(2)}) copy-start(s32[128]{0:T(128)} %owner_ref.1) | copy-start | bytes 1540
  44.5 24.5 %all-gather.3.cloned.1.call-start = ((), (), s32[]{:S(2)}) async-start(), calls=%async_computation.4 | async-start | bytes 1572864 | tf_op jit(solution)/shard_map/all_gather | solution.py:216
  69.0 1.2 copy-start.4
  74.3 1.3 copy-start
  89.8 58.5 %copy-start.5 = (bf16[2,2,256,256]{3,2,1,0:T(8,128)(2,1)S(1)}, bf16[2,2,256,256]{3,2,1,0:T(8,128)(2,1)}, u32[]{:S(2)}) copy-start(bf16[2,2,256,256]{3,2,1,0:T(8,128)(2,1)} %psf_ref.1) | copy-start | bytes 1572868
Sparse Core Ops, SparseCore 0:
  46.9 22.0 all-gather.2
